TPU v7x, 32 devices: a whole 2x2x4 slice. The times are simulated.
32 devices in a mesh: groups: 2 (over x), pool: 16 (over z, y, core).
Axes of the slice: x: 2, y: 2, z: 4, core: 2. Of those that a mesh axis runs over, the one named last changes fastest.
Arguments:
- queries: bfloat16 [1024, 16384], P(None, ('groups', 'pool')), parts along dimension 1, may hold values from -80 to 80
- stretch_keys: bfloat16 [16384, 128], P(('groups', 'pool')), parts along dimension 0, may hold values from -6 to 6
- stretch_values: bfloat16 [16384, 128], P(('groups', 'pool')), parts along dimension 0, may hold values from -6 to 6
- pool_keys: bfloat16 [96, 256, 128], P(('groups', 'pool')), parts along dimension 0, may hold values from -8 to 8
- pool_values: bfloat16 [96, 256, 128], P(('groups', 'pool')), parts along dimension 0, may hold values from -6 to 6
- page_counts: int32 [4], P('groups'), parts along dimension 0, may hold values from 1 to 11, as said below
- page_table: int32 [4, 4, 11], P('groups'), parts along dimension 0, may hold values from -1 to 47, as said below
Outputs:
- attended: bfloat16 [1024, 16384], P(None, ('groups', 'pool')), parts along dimension 1
There are 2 independent parts, one for each index of `groups`. A program takes and returns all parts, laid end to end along the dimension named above; each array names one. Nothing has to cross between parts.
Inputs may be any that keep to these rules, and one draw needn't show every extreme that they name: `page_counts`: the counts sum to 12; the largest is exactly 11. `page_table`: entry [r, g, j] with j < page_counts[r] is the slot of pool_keys and pool_values holding page j of request r for key head g; slot s lies on device s // 3 of the pool axis. Other entries are -1. Every slot is named exactly once. No device holds two slots named by the same r and g.
All inputs are finite; a program needn't handle non-finite values.
Results may differ from a plain program's by a relative error of at most 0.0055.
Values may be sent and summed in bfloat16 or wider, within the bound.
No kernel may reach another device: no remote copies, remote signals or barrier semaphores. Data moves between devices by JAX's collectives and lax.ppermute only.
A program may use at most 64 MiB of HBM per device.

v0:
```python
import math

import jax
import jax.numpy as jnp
from jax import lax
from jax.sharding import PartitionSpec as P

HD = 128
QH = 32
KVH = 4
PAGE = 256
STRETCH = 1024
SLOTS_DEV = 3


def swapped(value, axis, distance):
    mask = 2**distance
    pairs = [(source, source ^ mask) for source in range(lax.axis_size(axis))]
    return lax.ppermute(value, axis, pairs)


def shards(queries, stretch_keys, stretch_values, pool_keys, pool_values, page_counts, page_table):
    own_index = lax.axis_index("pool")
    heads_here = queries.shape[1] // HD
    span_size = QH // heads_here
    sharers = span_size // KVH
    request = own_index // span_size
    kv_head = own_index % span_size // sharers
    half_index = own_index % sharers
    query_local = queries.reshape(STRETCH, heads_here, HD)
    score_scale = 1.0 / math.sqrt(HD)

    def advance(carry_state, key_block, value_block, visible):
        running_max, totals, accumulated = carry_state
        scores = (
            jnp.einsum("thd,kd->htk", query_local, key_block, preferred_element_type=jnp.float32)
            * score_scale
        )
        if visible is not None:
            scores = jnp.where(visible[None], scores, -jnp.inf)
        new_max = jnp.maximum(running_max, jnp.max(scores, axis=2))
        rescale = jnp.exp(running_max - new_max)
        weights = jnp.exp(scores - new_max[:, :, None])
        totals = totals * rescale + jnp.sum(weights, axis=2)
        accumulated = accumulated * rescale[:, :, None] + jnp.einsum(
            "htk,kd->htd",
            weights.astype(jnp.bfloat16),
            value_block,
            preferred_element_type=jnp.float32,
        )
        return (new_max, totals, accumulated)

    other_keys, other_values = swapped((stretch_keys, stretch_values), "pool", 0)
    lower_half = half_index == 0
    full_keys = jnp.where(
        lower_half,
        jnp.concatenate([stretch_keys, other_keys], 0),
        jnp.concatenate([other_keys, stretch_keys], 0),
    )
    full_values = jnp.where(
        lower_half,
        jnp.concatenate([stretch_values, other_values], 0),
        jnp.concatenate([other_values, stretch_values], 0),
    )
    carry_state = (
        jnp.full((heads_here, STRETCH), -jnp.inf, jnp.float32),
        jnp.zeros((heads_here, STRETCH), jnp.float32),
        jnp.zeros((heads_here, STRETCH, HD), jnp.float32),
    )
    positions = jnp.arange(STRETCH)
    for block_index in range(STRETCH // PAGE):
        key_block = full_keys[block_index * PAGE : (block_index + 1) * PAGE]
        value_block = full_values[block_index * PAGE : (block_index + 1) * PAGE]
        visible = (block_index * PAGE + jnp.arange(PAGE))[None, :] <= positions[:, None]
        carry_state = advance(carry_state, key_block, value_block, visible)
    flat_table = page_table.reshape(-1, page_table.shape[2])
    slot_row = lax.dynamic_index_in_dim(flat_table, request * KVH + kv_head, 0, keepdims=False)
    my_pages = page_counts[request]
    readers = jnp.arange(lax.axis_size("pool")) // sharers
    reader_rows = flat_table[readers]
    matched = reader_rows // SLOTS_DEV == own_index
    slot_of = jnp.sum(jnp.where(matched, reader_rows % SLOTS_DEV, 0), axis=1)
    sends = jnp.any(matched, axis=1)
    picker = ((slot_of[:, None] == jnp.arange(SLOTS_DEV)[None, :]) & sends[:, None]).astype(
        jnp.bfloat16
    )
    send_keys = jnp.einsum(
        "ns,spd->npd", picker, pool_keys, preferred_element_type=jnp.float32
    ).astype(jnp.bfloat16)
    send_values = jnp.einsum(
        "ns,spd->npd", picker, pool_values, preferred_element_type=jnp.float32
    ).astype(jnp.bfloat16)
    recv_keys, recv_values = (
        lax.all_to_all(send_keys, "pool", split_axis=0, concat_axis=0, tiled=True),
        lax.all_to_all(send_values, "pool", split_axis=0, concat_axis=0, tiled=True),
    )

    def page_step(page_index, inner_state):
        owner = slot_row[page_index] // SLOTS_DEV
        key_block = lax.dynamic_index_in_dim(recv_keys, owner, 0, keepdims=False)
        value_block = lax.dynamic_index_in_dim(recv_values, owner, 0, keepdims=False)
        return advance(inner_state, key_block, value_block, None)

    carry_state = lax.fori_loop(0, my_pages, page_step, carry_state)
    running_max, totals, accumulated = carry_state
    result = (accumulated / totals[:, :, None]).astype(jnp.bfloat16)
    return result.transpose(1, 0, 2).reshape(STRETCH, heads_here * HD)


def solution(mesh):
    placed = (
        P(None, ("groups", "pool")),
        P(("groups", "pool"), None),
        P(("groups", "pool"), None),
        P(("groups", "pool"), None, None),
        P(("groups", "pool"), None, None),
        P("groups"),
        P("groups", None, None),
    )
    return jax.shard_map(
        shards, mesh=mesh, in_specs=placed, out_specs=P(None, ("groups", "pool")), check_vma=False
    )
```

profile of v0, /device:TPU:16, one launch (start us, length us, event | category | flops | bytes accessed | tf_op | source)
XLA Modules:
  0.0 157.5 jit_solution(16215863665657653843)
XLA Ops:
  3.9 6.2 %all-to-all-start = ((bf16[16,256,128]{2,1,0:T(8,128)(2,1)}), bf16[16,256,128]{2,1,0:T(8,128)(2,1)}, u32[]{:S(2)}, u32[]{:S(2)}) async-start(bf16[16,256,128]{2,1,0:T(8,128)(2,1)} %copy.45), calls=%async_computation | async-start | bytes 2097152 | tf_op jit(solution)/shard_map/all_to_all | solution.py:94
  10.8 1.6 convolution_convert_fusion
  14.3 2.5 %copy.47 = bf16[16,256,128]{2,1,0:T(8,128)(2,1)} copy(bf16[16,256,128]{2,0,1:T(8,128)(2,1)} %convolution_convert_fusion) | data formatting | bytes 2097152 | tf_op jit(solution)/shard_map/convert_element_type | solution.py:92
  21.4 1.9 %fusion.18 = (f32[4,1024]{1,0:T(4,128)S(1)}, f32[4,1024]{1,0:T(4,128)S(1)}) fusion(f32[256,1024,4]{1,0,2:T(8,128)S(1)} %get-tuple-element.189, f32[4,1024]{1,0:T(4,128)S(1)} %get-tuple-element.188, pred[1024,256]{0,1:T(8,128)(4,1)S(1)} %iota_compare_fusion.3, f32[4,1024]{1,0:T(4,128)S(1)} %get-tuple-element.261, f32[256,1024,4]{1,0,2:T(8,128)S(1)} %get-tuple-element.185, ...), kind=kLoop, calls=%fused_computation.29 | loop fusion | flops 8380416 | bytes 8978432 | tf_op jit(solution)/shard_map/reduce_sum | solution.py:44
  24.3 1.9 %fusion.20 = (f32[4,1024]{1,0:T(4,128)S(1)}, f32[4,1024]{1,0:T(4,128)S(1)}) fusion(f32[256,1024,4]{1,0,2:T(8,128)S(1)} %get-tuple-element.191, f32[4,1024]{1,0:T(4,128)S(1)} %get-tuple-element.180, pred[1024,256]{0,1:T(8,128)(4,1)S(1)} %iota_compare_fusion.2, f32[4,1024]{1,0:T(4,128)S(1)} %get-tuple-element.179, f32[256,1024,4]{1,0,2:T(8,128)S(1)} %get-tuple-element.187, ...), kind=kLoop, calls=%fused_computation.31 | loop fusion | flops 8380416 | bytes 8978432 | tf_op jit(solution)/shard_map/reduce_sum | solution.py:44
  26.2 9.2 %all-to-all-done = bf16[16,256,128]{2,1,0:T(8,128)(2,1)} async-done(((bf16[16,256,128]{2,1,0:T(8,128)(2,1)}), bf16[16,256,128]{2,1,0:T(8,128)(2,1)}, u32[]{:S(2)}, u32[]{:S(2)}) %all-to-all-start) | async-done | bytes 1048608 | tf_op jit(solution)/shard_map/all_to_all | solution.py:94
  35.4 4.6 %all-to-all-start.1 = ((bf16[16,256,128]{2,1,0:T(8,128)(2,1)}), bf16[16,256,128]{2,1,0:T(8,128)(2,1)}, u32[]{:S(2)}, u32[]{:S(2)}) async-start(bf16[16,256,128]{2,1,0:T(8,128)(2,1)} %copy.47), calls=%async_computation.1 | async-start | bytes 2097152 | tf_op jit(solution)/shard_map/all_to_all | solution.py:95
  40.2 3.8 %fusion.29 = f32[4,1024,128]{2,1,0:T(8,128)S(1)} fusion(f32[256,1024,4]{1,0,2:T(8,128)} %copy-done.3, f32[4,1024]{1,0:T(4,128)S(1)} %get-tuple-element.261, pred[1024,256]{0,1:T(8,128)(4,1)S(1)} %iota_compare_fusion, bf16[1024,128]{1,0:T(8,128)(2,1)S(1)} %maximum_select_fusion.1), kind=kOutput, calls=%fused_computation.40 | convolution fusion | flops 272629760 | bytes 6635520 | tf_op jit(solution)/shard_map/htk,kd->htd/dot_general | solution.py:45
  48.3 3.1 %multiply_add_fusion.2 = f32[4,1024,128]{2,1,0:T(8,128)S(1)} fusion(f32[4,1024,128]{2,1,0:T(8,128)S(1)} %fusion.29, f32[4,1024,128]{2,1,0:T(8,128)S(1)} %fusion.31, f32[4,1024,128]{2,1,0:T(8,128)S(1)} %fusion.33, f32[256,1024,4]{1,0,2:T(8,128)S(1)} %copy-done.2, f32[4,1024]{1,0:T(4,128)S(1)} %get-tuple-element.188, pred[1024,256]{0,1:T(8,128)(4,1)S(1)} %copy-done.9, ...), kind=kOutput, calls=%fused_computation.45 | convolution fusion | flops 276299776 | bytes 12992512 | tf_op jit(solution)/shard_map/htk,kd->htd/dot_general | solution.py:45
  51.4 13.9 %all-to-all-done.1 = bf16[16,256,128]{2,1,0:T(8,128)(2,1)} async-done(((bf16[16,256,128]{2,1,0:T(8,128)(2,1)}), bf16[16,256,128]{2,1,0:T(8,128)(2,1)}, u32[]{:S(2)}, u32[]{:S(2)}) %all-to-all-start.1) | async-done | bytes 1048608 | tf_op jit(solution)/shard_map/all_to_all | solution.py:95
  65.3 90.7 %while.16 = (s32[]{:T(128)}, f32[4,1024]{1,0:T(4,128)S(1)}, f32[4,1024]{1,0:T(4,128)S(1)}, f32[4,1024,128]{2,1,0:T(8,128)S(1)}, s32[]{:T(128)}, /*index=5*/s32[1...) while((s32[]{:T(128)}, f32[4,1024]{1,0:T(4,128)S(1)}, ...), condition=%wide.region_13.14_spmd, body=%wide.region_10.13_spmd.sunk | while | flops 546316288 | bytes 18219340 | solution.py:104
  70.9 2.6 %multiply_add_fusion.7 = f32[4,1024,128]{2,1,0:T(8,128)S(1)} fusion(f32[4,1024,128]{2,1,0:T(8,128)S(1)} %get-tuple-element.280, f32[256,1024,4]{1,0,2:T(8,128)S(1)} %get-tuple-element.257, f32[4,1024]{1,0:T(4,128)S(1)} %max.61, f32[4,1024]{1,0:T(4,128)S(1)} %get-tuple-element.259, bf16[16,256,128]{2,1,0:T(8,128)(2,1)} %get-tuple-element.302, ...), kind=kOutput, calls=%fused_computation.7.clone.1 | convolution fusion | flops 272629760 | bytes 8486916 | tf_op jit(solution)/shard_map/while/body/htk,kd->htd/dot_general | solution.py:45
  76.7 1.6 bitcast_reduce_fusion.2
  79.1 2.6 %multiply_add_fusion.7 = f32[4,1024,128]{2,1,0:T(8,128)S(1)} fusion(f32[4,1024,128]{2,1,0:T(8,128)S(1)} %get-tuple-element.280, f32[256,1024,4]{1,0,2:T(8,128)S(1)} %get-tuple-element.257, f32[4,1024]{1,0:T(4,128)S(1)} %max.61, f32[4,1024]{1,0:T(4,128)S(1)} %get-tuple-element.259, bf16[16,256,128]{2,1,0:T(8,128)(2,1)} %get-tuple-element.302, ...), kind=kOutput, calls=%fused_computation.7.clone.1 | convolution fusion | flops 272629760 | bytes 8486916 | tf_op jit(solution)/shard_map/while/body/htk,kd->htd/dot_general | solution.py:45
  84.9 1.6 bitcast_reduce_fusion.2
  87.3 2.6 %multiply_add_fusion.7 = f32[4,1024,128]{2,1,0:T(8,128)S(1)} fusion(f32[4,1024,128]{2,1,0:T(8,128)S(1)} %get-tuple-element.280, f32[256,1024,4]{1,0,2:T(8,128)S(1)} %get-tuple-element.257, f32[4,1024]{1,0:T(4,128)S(1)} %max.61, f32[4,1024]{1,0:T(4,128)S(1)} %get-tuple-element.259, bf16[16,256,128]{2,1,0:T(8,128)(2,1)} %get-tuple-element.302, ...), kind=kOutput, calls=%fused_computation.7.clone.1 | convolution fusion | flops 272629760 | bytes 8486916 | tf_op jit(solution)/shard_map/while/body/htk,kd->htd/dot_general | solution.py:45
  93.1 1.6 bitcast_reduce_fusion.2
  95.4 2.6 %multiply_add_fusion.7 = f32[4,1024,128]{2,1,0:T(8,128)S(1)} fusion(f32[4,1024,128]{2,1,0:T(8,128)S(1)} %get-tuple-element.280, f32[256,1024,4]{1,0,2:T(8,128)S(1)} %get-tuple-element.257, f32[4,1024]{1,0:T(4,128)S(1)} %max.61, f32[4,1024]{1,0:T(4,128)S(1)} %get-tuple-element.259, bf16[16,256,128]{2,1,0:T(8,128)(2,1)} %get-tuple-element.302, ...), kind=kOutput, calls=%fused_computation.7.clone.1 | convolution fusion | flops 272629760 | bytes 8486916 | tf_op jit(solution)/shard_map/while/body/htk,kd->htd/dot_general | solution.py:45
  101.3 1.6 bitcast_reduce_fusion.2
  103.6 2.6 %multiply_add_fusion.7 = f32[4,1024,128]{2,1,0:T(8,128)S(1)} fusion(f32[4,1024,128]{2,1,0:T(8,128)S(1)} %get-tuple-element.280, f32[256,1024,4]{1,0,2:T(8,128)S(1)} %get-tuple-element.257, f32[4,1024]{1,0:T(4,128)S(1)} %max.61, f32[4,1024]{1,0:T(4,128)S(1)} %get-tuple-element.259, bf16[16,256,128]{2,1,0:T(8,128)(2,1)} %get-tuple-element.302, ...), kind=kOutput, calls=%fused_computation.7.clone.1 | convolution fusion | flops 272629760 | bytes 8486916 | tf_op jit(solution)/shard_map/while/body/htk,kd->htd/dot_general | solution.py:45
  109.5 1.6 bitcast_reduce_fusion.2
  111.8 2.6 %multiply_add_fusion.7 = f32[4,1024,128]{2,1,0:T(8,128)S(1)} fusion(f32[4,1024,128]{2,1,0:T(8,128)S(1)} %get-tuple-element.280, f32[256,1024,4]{1,0,2:T(8,128)S(1)} %get-tuple-element.257, f32[4,1024]{1,0:T(4,128)S(1)} %max.61, f32[4,1024]{1,0:T(4,128)S(1)} %get-tuple-element.259, bf16[16,256,128]{2,1,0:T(8,128)(2,1)} %get-tuple-element.302, ...), kind=kOutput, calls=%fused_computation.7.clone.1 | convolution fusion | flops 272629760 | bytes 8486916 | tf_op jit(solution)/shard_map/while/body/htk,kd->htd/dot_general | solution.py:45
  117.6 1.6 bitcast_reduce_fusion.2
  120.0 2.6 %multiply_add_fusion.7 = f32[4,1024,128]{2,1,0:T(8,128)S(1)} fusion(f32[4,1024,128]{2,1,0:T(8,128)S(1)} %get-tuple-element.280, f32[256,1024,4]{1,0,2:T(8,128)S(1)} %get-tuple-element.257, f32[4,1024]{1,0:T(4,128)S(1)} %max.61, f32[4,1024]{1,0:T(4,128)S(1)} %get-tuple-element.259, bf16[16,256,128]{2,1,0:T(8,128)(2,1)} %get-tuple-element.302, ...), kind=kOutput, calls=%fused_computation.7.clone.1 | convolution fusion | flops 272629760 | bytes 8486916 | tf_op jit(solution)/shard_map/while/body/htk,kd->htd/dot_general | solution.py:45
  125.8 1.6 bitcast_reduce_fusion.2
  128.2 2.6 %multiply_add_fusion.7 = f32[4,1024,128]{2,1,0:T(8,128)S(1)} fusion(f32[4,1024,128]{2,1,0:T(8,128)S(1)} %get-tuple-element.280, f32[256,1024,4]{1,0,2:T(8,128)S(1)} %get-tuple-element.257, f32[4,1024]{1,0:T(4,128)S(1)} %max.61, f32[4,1024]{1,0:T(4,128)S(1)} %get-tuple-element.259, bf16[16,256,128]{2,1,0:T(8,128)(2,1)} %get-tuple-element.302, ...), kind=kOutput, calls=%fused_computation.7.clone.1 | convolution fusion | flops 272629760 | bytes 8486916 | tf_op jit(solution)/shard_map/while/body/htk,kd->htd/dot_general | solution.py:45
  134.0 1.6 bitcast_reduce_fusion.2
  136.4 2.6 %multiply_add_fusion.7 = f32[4,1024,128]{2,1,0:T(8,128)S(1)} fusion(f32[4,1024,128]{2,1,0:T(8,128)S(1)} %get-tuple-element.280, f32[256,1024,4]{1,0,2:T(8,128)S(1)} %get-tuple-element.257, f32[4,1024]{1,0:T(4,128)S(1)} %max.61, f32[4,1024]{1,0:T(4,128)S(1)} %get-tuple-element.259, bf16[16,256,128]{2,1,0:T(8,128)(2,1)} %get-tuple-element.302, ...), kind=kOutput, calls=%fused_computation.7.clone.1 | convolution fusion | flops 272629760 | bytes 8486916 | tf_op jit(solution)/shard_map/while/body/htk,kd->htd/dot_general | solution.py:45
  142.2 1.6 bitcast_reduce_fusion.2
  144.5 2.6 %multiply_add_fusion.7 = f32[4,1024,128]{2,1,0:T(8,128)S(1)} fusion(f32[4,1024,128]{2,1,0:T(8,128)S(1)} %get-tuple-element.280, f32[256,1024,4]{1,0,2:T(8,128)S(1)} %get-tuple-element.257, f32[4,1024]{1,0:T(4,128)S(1)} %max.61, f32[4,1024]{1,0:T(4,128)S(1)} %get-tuple-element.259, bf16[16,256,128]{2,1,0:T(8,128)(2,1)} %get-tuple-element.302, ...), kind=kOutput, calls=%fused_computation.7.clone.1 | convolution fusion | flops 272629760 | bytes 8486916 | tf_op jit(solution)/shard_map/while/body/htk,kd->htd/dot_general | solution.py:45
  150.4 1.6 bitcast_reduce_fusion.2
  152.7 2.6 %multiply_add_fusion.7 = f32[4,1024,128]{2,1,0:T(8,128)S(1)} fusion(f32[4,1024,128]{2,1,0:T(8,128)S(1)} %get-tuple-element.280, f32[256,1024,4]{1,0,2:T(8,128)S(1)} %get-tuple-element.257, f32[4,1024]{1,0:T(4,128)S(1)} %max.61, f32[4,1024]{1,0:T(4,128)S(1)} %get-tuple-element.259, bf16[16,256,128]{2,1,0:T(8,128)(2,1)} %get-tuple-element.302, ...), kind=kOutput, calls=%fused_computation.7.clone.1 | convolution fusion | flops 272629760 | bytes 8486916 | tf_op jit(solution)/shard_map/while/body/htk,kd->htd/dot_general | solution.py:45
  (119 shorter events, 34.3 us)
Async XLA Ops:
  0.0 2.1 %copy-start = (bf16[3,256,128]{2,1,0:T(8,128)(2,1)S(1)}, bf16[3,256,128]{2,1,0:T(8,128)(2,1)}, u32[]{:S(2)}) copy-start(bf16[3,256,128]{2,1,0:T(8,128)(2,1)} %param.12) | copy-start | bytes 589828
  0.0 10.8 %copy-start.11 = (bf16[3,256,128]{2,1,0:T(8,128)(2,1)S(1)}, bf16[3,256,128]{2,1,0:T(8,128)(2,1)}, u32[]{:S(2)}) copy-start(bf16[3,256,128]{2,1,0:T(8,128)(2,1)} %param.13) | copy-start | bytes 589828
  0.0 13.1 %copy-start.10 = (bf16[1024,512]{1,0:T(8,128)(2,1)S(1)}, bf16[1024,512]{1,0:T(8,128)(2,1)}, u32[]{:S(2)}) copy-start(bf16[1024,512]{1,0:T(8,128)(2,1)} %param.9) | copy-start | bytes 3145732
  0.0 17.5 %collective-permute-start = (bf16[512,128]{1,0:T(8,128)(2,1)}, bf16[512,128]{1,0:T(8,128)(2,1)S(1)}, u32[]{:S(2)}, u32[]{:S(2)}) collective-permute-start(bf16[512,128]{1,0:T(8,128)(2,1)} %param.10), channel_id=1, source_target_pairs={{0,1},{1,0},{2,3},{3,2},{4,5},{5,4},{6,7},{7,6},{8,9},{9,8},{10,11... | collective-permute-start | bytes 393224 | tf_op jit(solution)/shard_map/ppermute | solution.py:19
  0.1 40.0 %collective-permute-start.1 = (bf16[512,128]{1,0:T(8,128)(2,1)}, bf16[512,128]{1,0:T(8,128)(2,1)S(1)}, u32[]{:S(2)}, u32[]{:S(2)}) collective-permute-start(bf16[512,128]{1,0:T(8,128)(2,1)} %param.11), channel_id=1, source_target_pairs={{0,1},{1,0},{2,3},{3,2},{4,5},{5,4},{6,7},{7,6},{8,9},{9,8},{10,11... | collective-permute-start | bytes 393224 | tf_op jit(solution)/shard_map/ppermute | solution.py:19
  3.9 31.5 %all-to-all-start = ((bf16[16,256,128]{2,1,0:T(8,128)(2,1)}), bf16[16,256,128]{2,1,0:T(8,128)(2,1)}, u32[]{:S(2)}, u32[]{:S(2)}) async-start(bf16[16,256,128]{2,1,0:T(8,128)(2,1)} %copy.45), calls=%async_computation | async-start | bytes 2097152 | tf_op jit(solution)/shard_map/all_to_all | solution.py:94
  10.2 6.7 %copy-start.14 = (s32[2]{0:T(128)S(1)}, s32[2]{0:T(128)}, u32[]{:S(2)}) copy-start(s32[2]{0:T(128)} %param.14) | copy-start | bytes 28
  10.4 7.2 %copy-start.12 = (bf16[512,128]{1,0:T(8,128)(2,1)S(1)}, bf16[512,128]{1,0:T(8,128)(2,1)}, u32[]{:S(2)}) copy-start(bf16[512,128]{1,0:T(8,128)(2,1)} %param.10) | copy-start | bytes 393220
  17.5 3.9 %copy-start.8 = (pred[1024,256]{0,1:T(8,128)(4,1)}, pred[1024,256]{0,1:T(8,128)(4,1)S(1)}, u32[]{:S(2)}) copy-start(pred[1024,256]{0,1:T(8,128)(4,1)S(1)} %iota_compare_fusion.3) | copy-start | bytes 786436
  18.6 2.8 %copy-start.3 = (f32[256,1024,4]{1,0,2:T(8,128)}, f32[256,1024,4]{1,0,2:T(8,128)S(1)}, u32[]{:S(2)}) copy-start(f32[256,1024,4]{1,0,2:T(8,128)S(1)} %get-tuple-element.185) | copy-start | bytes 12582916
  19.5 3.8 %copy-start.4 = (f32[256,1024,4]{1,0,2:T(8,128)}, f32[256,1024,4]{1,0,2:T(8,128)S(1)}, u32[]{:S(2)}) copy-start(f32[256,1024,4]{1,0,2:T(8,128)S(1)} %get-tuple-element.187) | copy-start | bytes 12582916
  20.5 2.9 %copy-start.1 = (f32[256,1024,4]{1,0,2:T(8,128)}, f32[256,1024,4]{1,0,2:T(8,128)S(1)}, u32[]{:S(2)}) copy-start(f32[256,1024,4]{1,0,2:T(8,128)S(1)} %get-tuple-element.189) | copy-start | bytes 12582916
  21.4 2.9 %copy-start.6 = (f32[256,1024,4]{1,0,2:T(8,128)}, f32[256,1024,4]{1,0,2:T(8,128)S(1)}, u32[]{:S(2)}) copy-start(f32[256,1024,4]{1,0,2:T(8,128)S(1)} %get-tuple-element.191) | copy-start | bytes 12582916
  24.3 15.8 %copy-start.13 = (bf16[512,128]{1,0:T(8,128)(2,1)S(1)}, bf16[512,128]{1,0:T(8,128)(2,1)}, u32[]{:S(2)}) copy-start(bf16[512,128]{1,0:T(8,128)(2,1)} %param.11) | copy-start | bytes 393220
  35.4 29.9 %all-to-all-start.1 = ((bf16[16,256,128]{2,1,0:T(8,128)(2,1)}), bf16[16,256,128]{2,1,0:T(8,128)(2,1)}, u32[]{:S(2)}, u32[]{:S(2)}) async-start(bf16[16,256,128]{2,1,0:T(8,128)(2,1)} %copy.47), calls=%async_computation.1 | async-start | bytes 2097152 | tf_op jit(solution)/shard_map/all_to_all | solution.py:95
  40.0 3.9 %copy-start.5 = (f32[256,1024,4]{1,0,2:T(8,128)S(1)}, f32[256,1024,4]{1,0,2:T(8,128)}, u32[]{:S(2)}) copy-start(f32[256,1024,4]{1,0,2:T(8,128)} %copy-done.4) | copy-start | bytes 12582916
  43.9 2.2 %copy-start.7 = (f32[256,1024,4]{1,0,2:T(8,128)S(1)}, f32[256,1024,4]{1,0,2:T(8,128)}, u32[]{:S(2)}) copy-start(f32[256,1024,4]{1,0,2:T(8,128)} %copy-done.6) | copy-start | bytes 12582916
  46.1 2.2 %copy-start.2 = (f32[256,1024,4]{1,0,2:T(8,128)S(1)}, f32[256,1024,4]{1,0,2:T(8,128)}, u32[]{:S(2)}) copy-start(f32[256,1024,4]{1,0,2:T(8,128)} %copy-done.1) | copy-start | bytes 12582916
  46.1 2.2 %copy-start.9 = (pred[1024,256]{0,1:T(8,128)(4,1)S(1)}, pred[1024,256]{0,1:T(8,128)(4,1)}, u32[]{:S(2)}) copy-start(pred[1024,256]{0,1:T(8,128)(4,1)} %copy-done.8) | copy-start | bytes 786436
where the time goes:
time: 159 us; the launch traced here: 158 us
  matrix products  61 us (38%)
  loops' own time  30.5 us (19%)
  waiting for transfers between devices  23.1 us (15%)
  local copies, waits for them, and re-layouts  16.5 us (10%)
  other arithmetic  14.7 us (9%)
  starting transfers between devices  11.4 us (7%)
    dot_general x15, matrix products, advance(): jnp.einsum('htk,kd->htd', weights.astype(jnp.bfloat16), value_block, pref...  38 us
    another operation x1, loops' own time, shards(): carry_state = lax.fori_loop(0, my_pages, page_step, carry_state)  30.5 us
    dot_general x15, matrix products, advance(): jnp.einsum('thd,kd->htk', query_local, key_block, preferred_element_type=...  20.9 us
    all_to_all x1, waiting for transfers between devices, shards(): lax.all_to_all(send_values, 'pool', split_axis=0, concat_axis=0, tiled=True)  13.9 us
    reduce_sum x13, other arithmetic, advance(): totals = totals * rescale + jnp.sum(weights, axis=2)  11.7 us
    all_to_all x1, waiting for transfers between devices, shards(): lax.all_to_all(send_keys, 'pool', split_axis=0, concat_axis=0, tiled=True)  9.19 us
    dynamic_slice x11, local copies, waits for them, and re-layouts, page_step(): owner = slot_row[page_index] // SLOTS_DEV  6.46 us
    all_to_all x1, starting transfers between devices, shards(): lax.all_to_all(send_keys, 'pool', split_axis=0, concat_axis=0, tiled=True)  6.18 us
  transfers between devices with their start and end apart: 4, of which 2 were waited for; matrix products, arithmetic and copies ran while one was open for 18% of the time, Pallas kernels for 0%

commit v1 on v0

v1 whole, which is shorter than its diff:
```python
import functools
import math

import jax
import jax.numpy as jnp
from jax import lax
from jax.experimental import pallas as pl
from jax.experimental.pallas import tpu as pltpu
from jax.sharding import PartitionSpec as P

HD = 128
QH = 32
KVH = 4
PAGE = 256
STRETCH = 1024
SLOTS_DEV = 3
CORES = 2
TILE = 256
VMEM_BYTES = 24 * 2**20
EXP2_SCALE = math.log2(math.e) / math.sqrt(HD)
ROW_BY_ROW = (((1,), (1,)), ((), ()))

SMEM = pl.BlockSpec(memory_space=pltpu.SMEM)
ANY = pl.BlockSpec(memory_space=pl.ANY)


def swapped(value, axis, mask):
    pairs = [(source, source ^ mask) for source in range(lax.axis_size(axis))]
    return lax.ppermute(value, axis, pairs)


def pick_kernel(offsets, own_ref, table_ref, keys_ref, values_ref, *refs):
    outs, sem = refs[:-1], refs[-1]
    own = own_ref[0]
    first = own * SLOTS_DEV
    depth = table_ref.shape[1]
    copies = []
    for at, offset in enumerate(offsets):
        row = jnp.bitwise_xor(own // CORES, offset)

        def look(page, slot, row=row):
            there = table_ref[row, page] - first
            return jnp.where((there >= 0) & (there < SLOTS_DEV), there, slot)

        slot = lax.fori_loop(0, depth, look, 0, unroll=True)
        for side, source in enumerate((keys_ref, values_ref)):
            copy = pltpu.make_async_copy(source.at[slot], outs[at].at[side], sem.at[at, side])
            copy.start()
            copies.append(copy)
    for copy in copies:
        copy.wait()


def pick(own, table, keys, values, offsets):
    return pl.pallas_call(
        functools.partial(pick_kernel, offsets),
        out_shape=[jax.ShapeDtypeStruct((2, PAGE, HD), keys.dtype)] * len(offsets),
        in_specs=[SMEM, SMEM, ANY, ANY],
        out_specs=[ANY] * len(offsets),
        scratch_shapes=[pltpu.SemaphoreType.DMA((len(offsets), 2))],
        compiler_params=pltpu.CompilerParams(vmem_limit_bytes=VMEM_BYTES),
        name="pick",
    )(own, table, keys, values)


def online(scores, values, old_max, old_totals, old_acc):
    width = scores.shape[1] // HD
    peak = jnp.max(scores, axis=1, keepdims=True)
    new_max = jnp.broadcast_to(peak, (scores.shape[0], HD))
    if old_max is not None:
        new_max = jnp.maximum(old_max, new_max)
    weights = jnp.exp2((scores - jnp.concatenate([new_max] * width, 1)) * EXP2_SCALE)
    totals = weights[:, :HD]
    for part in range(1, width):
        totals = totals + weights[:, part * HD : (part + 1) * HD]
    acc = jnp.dot(weights.astype(jnp.bfloat16), values, preferred_element_type=jnp.float32)
    if old_max is not None:
        rescale = jnp.exp2((old_max - new_max) * EXP2_SCALE)
        totals = old_totals * rescale + totals
        acc = old_acc * rescale + acc
    return new_max, totals, acc


def score(query, keys):
    return lax.dot_general(query, keys, ROW_BY_ROW, preferred_element_type=jnp.float32)


def stretch_kernel(own_ref, q_ref, k_ref, k2_ref, v_ref, v2_ref, m_ref, l_ref, a_ref, ks, vs, sem):
    @pl.when(pl.program_id(0) == 0)
    def _():
        half = own_ref[0] % CORES
        rows = k_ref.shape[0]
        copies = []
        for at, (source, target) in enumerate(((k_ref, ks), (k2_ref, ks), (v_ref, vs), (v2_ref, vs))):
            place = half if at % 2 == 0 else 1 - half
            start = pl.multiple_of(place * rows, rows)
            copies.append(pltpu.make_async_copy(source, target.at[pl.ds(start, rows)], sem.at[at]))
            copies[-1].start()
        for copy in copies:
            copy.wait()

    tiles = STRETCH // TILE
    row = lax.broadcasted_iota(jnp.int32, (TILE, TILE), 0)
    column = lax.broadcasted_iota(jnp.int32, (TILE, TILE), 1)

    def scores_of(tile):
        here = slice(tile * TILE, (tile + 1) * TILE)
        scores = score(q_ref[here, :], ks[: (tile + 1) * TILE])
        last = jnp.where(column <= row, scores[:, tile * TILE :], -jnp.inf)
        if tile == 0:
            return last
        return jnp.concatenate([scores[:, : tile * TILE], last], 1)

    order = list(range(tiles))[::-1]
    ahead = scores_of(order[0])
    for at, tile in enumerate(order):
        scores = ahead
        if at + 1 < tiles:
            ahead = scores_of(order[at + 1])
        here = slice(tile * TILE, (tile + 1) * TILE)
        m, l, a = online(scores, vs[: (tile + 1) * TILE], None, None, None)
        m_ref[0, here, :] = m
        l_ref[0, here, :] = l
        a_ref[0, here, :] = a


def pages_kernel(
    low, high, final, own_ref, table_ref, counts_ref, q_ref, near_ref, far_ref, m_in, l_in, a_in, *refs
):
    if final:
        o_ref, ks, vs, fill, m_ref, l_ref, a_ref, sem = refs
    else:
        m_ref, l_ref, a_ref, ks, vs, fill, sem = refs
    own = own_ref[0]
    chip = own // CORES
    core = own % CORES

    def copies(page):
        slot = jnp.maximum(table_ref[chip, page], 0)
        device = slot // SLOTS_DEV
        offset = jnp.bitwise_xor(device // CORES, chip)
        inside = (table_ref[chip, page] >= 0) & (offset >= low) & (offset < high)
        return inside, device % CORES == core, jnp.clip(offset - low, 0, high - low - 1)

    @pl.when(pl.program_id(0) == 0)
    def _():
        depth = table_ref.shape[1]

        def begin(page, filled):
            inside, mine, at = copies(page)

            @pl.when(inside & mine)
            def _():
                pltpu.make_async_copy(near_ref.at[at, 0], ks.at[filled], sem.at[filled, 0]).start()
                pltpu.make_async_copy(near_ref.at[at, 1], vs.at[filled], sem.at[filled, 1]).start()

            @pl.when(inside & jnp.logical_not(mine))
            def _():
                pltpu.make_async_copy(far_ref.at[at, 0], ks.at[filled], sem.at[filled, 0]).start()
                pltpu.make_async_copy(far_ref.at[at, 1], vs.at[filled], sem.at[filled, 1]).start()

            return filled + inside.astype(jnp.int32)

        filled = lax.fori_loop(0, depth, begin, 0)
        fill[0] = filled

        def end(at, _):
            pltpu.make_async_copy(near_ref.at[0, 0], ks.at[at], sem.at[at, 0]).wait()
            pltpu.make_async_copy(near_ref.at[0, 1], vs.at[at], sem.at[at, 1]).wait()
            return 0

        lax.fori_loop(0, filled, end, 0)

    for target, source in ((m_ref, m_in), (l_ref, l_in), (a_ref, a_in)):
        target[0] = source[0]
    filled = fill[0]
    tiles = STRETCH // TILE

    def block(first, pages):
        rows = pages * PAGE
        keys = ks[pl.ds(first, pages)].reshape(rows, HD)
        values = vs[pl.ds(first, pages)].reshape(rows, HD)
        ahead = score(q_ref[:TILE, :], keys)
        for tile in range(tiles):
            scores = ahead
            if tile + 1 < tiles:
                ahead = score(q_ref[(tile + 1) * TILE : (tile + 2) * TILE, :], keys)
            here = slice(tile * TILE, (tile + 1) * TILE)
            m, l, a = online(scores, values, m_ref[0, here, :], l_ref[0, here, :], a_ref[0, here, :])
            m_ref[0, here, :] = m
            l_ref[0, here, :] = l
            a_ref[0, here, :] = a

    def fours(at, _):
        block(at * 4, 4)
        return 0

    lax.fori_loop(0, filled // 4, fours, 0)

    @pl.when(filled % 4 >= 2)
    def _():
        block(filled // 4 * 4, 2)

    @pl.when(filled % 2 == 1)
    def _():
        block(filled - 1, 1)

    if final:
        for tile in range(tiles):
            here = slice(tile * TILE, (tile + 1) * TILE)
            totals = jnp.sum(l_ref[0, here, :], axis=1, keepdims=True)
            o_ref[here, :] = (a_ref[0, here, :] / totals).astype(o_ref.dtype)


def shards(queries, stretch_keys, stretch_values, pool_keys, pool_values, page_counts, page_table):
    own_index = lax.axis_index("pool")
    heads = queries.shape[1] // HD
    chips = lax.axis_size("pool") // CORES
    own = own_index.astype(jnp.int32).reshape(1)
    depth = page_table.shape[2]
    table = page_table.reshape(-1, depth)
    far_first = list(range(chips))[::-1]
    picked = dict(zip(far_first, pick(own, table, pool_keys, pool_values, far_first)))

    other_keys = swapped(stretch_keys, "pool", 1)
    other_values = swapped(stretch_values, "pool", 1)
    params = pltpu.CompilerParams(vmem_limit_bytes=VMEM_BYTES)
    q_spec = pl.BlockSpec((STRETCH, HD), lambda h: (0, h))
    s_spec = pl.BlockSpec((1, STRETCH, HD), lambda h: (h, 0, 0))
    s_shape = jax.ShapeDtypeStruct((heads, STRETCH, HD), jnp.float32)
    state = pl.pallas_call(
        stretch_kernel,
        grid=(heads,),
        out_shape=[s_shape] * 3,
        in_specs=[SMEM, q_spec, ANY, ANY, ANY, ANY],
        out_specs=[s_spec] * 3,
        scratch_shapes=[
            pltpu.VMEM((STRETCH, HD), jnp.bfloat16),
            pltpu.VMEM((STRETCH, HD), jnp.bfloat16),
            pltpu.SemaphoreType.DMA((4,)),
        ],
        compiler_params=params,
        cost_estimate=pl.CostEstimate(flops=4 * 10**9, bytes_accessed=8 * 10**6, transcendentals=0),
        name="stretch",
    )(own, queries, stretch_keys, other_keys, stretch_values, other_values)

    cut = chips * 3 // 4
    for low, high in ((0, cut), (cut, chips)):
        final = high == chips
        got = [picked[at] if at == 0 else swapped(picked[at], "pool", at * CORES) for at in range(low, high)]
        mine = jnp.stack(got)
        others = swapped(mine, "pool", 1)
        most = min(depth, CORES * (high - low))
        scratch = [
            pltpu.VMEM((most, PAGE, HD), jnp.bfloat16),
            pltpu.VMEM((most, PAGE, HD), jnp.bfloat16),
            pltpu.SMEM((1,), jnp.int32),
        ]
        if final:
            scratch += [pltpu.VMEM((1, STRETCH, HD), jnp.float32)] * 3
        scratch.append(pltpu.SemaphoreType.DMA((most, 2)))
        state = pl.pallas_call(
            functools.partial(pages_kernel, low, high, final),
            grid=(heads,),
            out_shape=jax.ShapeDtypeStruct(queries.shape, queries.dtype) if final else [s_shape] * 3,
            in_specs=[SMEM, SMEM, SMEM, q_spec, ANY, ANY, s_spec, s_spec, s_spec],
            out_specs=q_spec if final else [s_spec] * 3,
            scratch_shapes=scratch,
            compiler_params=params,
            cost_estimate=pl.CostEstimate(flops=4 * 10**9, bytes_accessed=8 * 10**6, transcendentals=0),
            name="pages",
        )(own, table, page_counts, queries, mine, others, *state)
    return state


def solution(mesh):
    placed = (
        P(None, ("groups", "pool")),
        P(("groups", "pool"), None),
        P(("groups", "pool"), None),
        P(("groups", "pool"), None, None),
        P(("groups", "pool"), None, None),
        P("groups"),
        P("groups", None, None),
    )
    return jax.shard_map(
        shards, mesh=mesh, in_specs=placed, out_specs=P(None, ("groups", "pool")), check_vma=False
    )
```

time: 159 us -> 68.4 us (0.43)
  the two profiles are of different devices: /device:TPU:16 before, /device:TPU:11 now
where the time goes in v1:
time: 68.4 us; the launch traced here: 68.9 us
  Pallas kernels  33.5 us (49%)
  waiting for transfers between devices  20.3 us (30%)
  starting transfers between devices  12.2 us (18%)
  local copies, waits for them, and re-layouts  2.67 us (4%)
    pallas_call x2, Pallas kernels, shards(): pl.pallas_call(functools.partial(pages_kernel, low, high, final), grid=(h...  25.9 us
    ppermute x11, waiting for transfers between devices, swapped(): return lax.ppermute(value, axis, pairs)  20.3 us
    ppermute x11, starting transfers between devices, swapped(): return lax.ppermute(value, axis, pairs)  12.2 us
    pallas_call x1, Pallas kernels, shards(): pl.pallas_call(stretch_kernel, grid=(heads,), out_shape=[s_shape] * 3, in...  5.34 us
    unnamed x21, local copies, waits for them, and re-layouts  2.65 us
    pallas_call x1, Pallas kernels, pick(): pl.pallas_call(functools.partial(pick_kernel, offsets), out_shape=[jax.Sh...  2.31 us
  transfers between devices with their start and end apart: 11, of which 5 were waited for; matrix products, arithmetic and copies ran while one was open for 0% of the time, Pallas kernels for 30%

profile of v1, /device:TPU:11, one launch (start us, length us, event | category | flops | bytes accessed | tf_op | source)
XLA Modules:
  0.0 68.9 jit_solution(15116438858688144410)
XLA Ops:
  0.0 0.9 %copy-done = bf16[3,256,128]{2,1,0:T(8,128)(2,1)S(1)} copy-done((bf16[3,256,128]{2,1,0:T(8,128)(2,1)S(1)}, bf16[3,256,128]{2,1,0:T(8,128)(2,1)}, u32[]{:S(2)}) %copy-start) | copy-done | bytes 196632
  0.9 0.9 %copy-done.1 = bf16[3,256,128]{2,1,0:T(8,128)(2,1)S(1)} copy-done((bf16[3,256,128]{2,1,0:T(8,128)(2,1)S(1)}, bf16[3,256,128]{2,1,0:T(8,128)(2,1)}, u32[]{:S(2)}) %copy-start.1) | copy-done | bytes 196632
  1.9 0.7 copy-done.2
  2.5 2.3 %pick.1 = (bf16[2,256,128]{2,1,0:T(8,128)(2,1)S(1)}, bf16[2,256,128]{2,1,0:T(8,128)(2,1)S(1)}, bf16[2,256,128]{2,1,0:T(8,128)(2,1)S(1)}, bf16[2,256,128]{2,1,0:T...) custom-call(s32[1]{0:T(128)} %bitcast.own_ref, ...), custom_call_target="tpu_custom_call" | custom-call | tf_op jit(solution)/shard_map/pick/pallas_call | solution.py:55
  4.9 1.3 %collective-permute-start.3 = (bf16[2,256,128]{2,1,0:T(8,128)(2,1)S(1)}, bf16[2,256,128]{2,1,0:T(8,128)(2,1)S(1)}, u32[]{:S(2)}, u32[]{:S(2)}) collective-permute-start(bf16[2,256,128]{2,1,0:T(8,128)(2,1)S(1)} %get-tuple-element.22), channel_id=1, source_target_pairs={{0,2},{1,3},{2,0},{3,1},{4,6},{5,7},{6,4},{7,5},{8,10},{9,11},{10,... | collective-permute-start | bytes 393224 | tf_op jit(solution)/shard_map/ppermute | solution.py:29
  6.2 0.2 collective-permute-start.4
  6.3 1.2 %collective-permute-start.5 = (bf16[2,256,128]{2,1,0:T(8,128)(2,1)S(1)}, bf16[2,256,128]{2,1,0:T(8,128)(2,1)S(1)}, u32[]{:S(2)}, u32[]{:S(2)}) collective-permute-start(bf16[2,256,128]{2,1,0:T(8,128)(2,1)S(1)} %get-tuple-element.24), channel_id=1, source_target_pairs={{0,6},{1,7},{2,4},{3,5},{4,2},{5,3},{6,0},{7,1},{8,14},{9,15},{10,... | collective-permute-start | bytes 393224 | tf_op jit(solution)/shard_map/ppermute | solution.py:29
  7.6 2.3 %collective-permute-start.6 = (bf16[2,256,128]{2,1,0:T(8,128)(2,1)S(1)}, bf16[2,256,128]{2,1,0:T(8,128)(2,1)S(1)}, u32[]{:S(2)}, u32[]{:S(2)}) collective-permute-start(bf16[2,256,128]{2,1,0:T(8,128)(2,1)S(1)} %get-tuple-element.25), channel_id=1, source_target_pairs={{0,8},{1,9},{2,10},{3,11},{4,12},{5,13},{6,14},{7,15},{8,0},{9,1},... | collective-permute-start | bytes 393224 | tf_op jit(solution)/shard_map/ppermute | solution.py:29
  9.9 1.0 %collective-permute-start.7 = (bf16[2,256,128]{2,1,0:T(8,128)(2,1)S(1)}, bf16[2,256,128]{2,1,0:T(8,128)(2,1)S(1)}, u32[]{:S(2)}, u32[]{:S(2)}) collective-permute-start(bf16[2,256,128]{2,1,0:T(8,128)(2,1)S(1)} %get-tuple-element.26), channel_id=1, source_target_pairs={{0,10},{1,11},{2,8},{3,9},{4,14},{5,15},{6,12},{7,13},{8,2},{9,3},... | collective-permute-start | bytes 393224 | tf_op jit(solution)/shard_map/ppermute | solution.py:29
  10.9 0.0 collective-permute-done.3
  11.0 0.0 collective-permute-done.4
  11.0 4.0 %collective-permute-done.5 = bf16[2,256,128]{2,1,0:T(8,128)(2,1)S(1)} collective-permute-done((bf16[2,256,128]{2,1,0:T(8,128)(2,1)S(1)}, bf16[2,256,128]{2,1,0:T(8,128)(2,1)S(1)}, u32[]{:S(2)}, u32[]{:S(2)}) %collective-permute-start.5) | collective-permute-done | bytes 131104 | tf_op jit(solution)/shard_map/ppermute | solution.py:29
  15.0 1.6 %collective-permute-done.6 = bf16[2,256,128]{2,1,0:T(8,128)(2,1)S(1)} collective-permute-done((bf16[2,256,128]{2,1,0:T(8,128)(2,1)S(1)}, bf16[2,256,128]{2,1,0:T(8,128)(2,1)S(1)}, u32[]{:S(2)}, u32[]{:S(2)}) %collective-permute-start.6) | collective-permute-done | bytes 131104 | tf_op jit(solution)/shard_map/ppermute | solution.py:29
  16.6 3.4 %collective-permute-done.7 = bf16[2,256,128]{2,1,0:T(8,128)(2,1)S(1)} collective-permute-done((bf16[2,256,128]{2,1,0:T(8,128)(2,1)S(1)}, bf16[2,256,128]{2,1,0:T(8,128)(2,1)S(1)}, u32[]{:S(2)}, u32[]{:S(2)}) %collective-permute-start.7) | collective-permute-done | bytes 131104 | tf_op jit(solution)/shard_map/ppermute | solution.py:29
  20.0 2.2 %collective-permute-start.8 = (bf16[6,2,256,128]{3,2,1,0:T(8,128)(2,1)S(1)}, bf16[6,2,256,128]{3,2,1,0:T(8,128)(2,1)S(1)}, u32[]{:S(2)}, u32[]{:S(2)}) collective-permute-start(bf16[6,2,256,128]{3,2,1,0:T(8,128)(2,1)S(1)} %bitcast_dynamic-update-slice_fusion.near_ref), channel_id=1, source_target_pairs={{0,1},{1,0},{2,3},{3,2},{4,5},{5,4},{6,7},{7,6},{8,9},{9,8},{10,11... | collective-permute-start | bytes 2359304 | tf_op jit(solution)/shard_map/ppermute | solution.py:29
  22.2 0.0 collective-permute-start
  22.2 2.4 %collective-permute-start.1 = (bf16[2,256,128]{2,1,0:T(8,128)(2,1)S(1)}, bf16[2,256,128]{2,1,0:T(8,128)(2,1)S(1)}, u32[]{:S(2)}, u32[]{:S(2)}) collective-permute-start(bf16[2,256,128]{2,1,0:T(8,128)(2,1)S(1)} %get-tuple-element.20), channel_id=1, source_target_pairs={{0,14},{1,15},{2,12},{3,13},{4,10},{5,11},{6,8},{7,9},{8,6},{9,7},... | collective-permute-start | bytes 393224 | tf_op jit(solution)/shard_map/ppermute | solution.py:29
  24.6 0.6 collective-permute-start.10
  25.2 0.0 collective-permute-start.9
  25.2 2.1 %collective-permute-done = bf16[2,256,128]{2,1,0:T(8,128)(2,1)S(1)} collective-permute-done((bf16[2,256,128]{2,1,0:T(8,128)(2,1)S(1)}, bf16[2,256,128]{2,1,0:T(8,128)(2,1)S(1)}, u32[]{:S(2)}, u32[]{:S(2)}) %collective-permute-start) | collective-permute-done | bytes 131104 | tf_op jit(solution)/shard_map/ppermute | solution.py:29
  27.2 9.3 %collective-permute-done.1 = bf16[2,256,128]{2,1,0:T(8,128)(2,1)S(1)} collective-permute-done((bf16[2,256,128]{2,1,0:T(8,128)(2,1)S(1)}, bf16[2,256,128]{2,1,0:T(8,128)(2,1)S(1)}, u32[]{:S(2)}, u32[]{:S(2)}) %collective-permute-start.1) | collective-permute-done | bytes 131104 | tf_op jit(solution)/shard_map/ppermute | solution.py:29
  36.6 0.0 copy-start.3
  36.6 0.0 copy-start.7
  36.6 0.9 %collective-permute-start.2 = (bf16[2,2,256,128]{3,2,1,0:T(8,128)(2,1)S(1)}, bf16[2,2,256,128]{3,2,1,0:T(8,128)(2,1)S(1)}, u32[]{:S(2)}, u32[]{:S(2)}) collective-permute-start(bf16[2,2,256,128]{3,2,1,0:T(8,128)(2,1)S(1)} %pad_maximum_fusion.near_ref), channel_id=1, source_target_pairs={{0,1},{1,0},{2,3},{3,2},{4,5},{5,4},{6,7},{7,6},{8,9},{9,8},{10,11... | collective-permute-start | bytes 786440 | tf_op jit(solution)/shard_map/ppermute | solution.py:29
  37.5 0.0 collective-permute-done.10.v2_ref
  37.6 0.0 collective-permute-done.9.k2_ref
  37.6 0.0 copy-done.4
  37.6 5.3 %stretch.1 = (f32[4,1024,128]{2,1,0:T(8,128)S(1)}, f32[4,1024,128]{2,1,0:T(8,128)S(1)}, f32[4,1024,128]{2,1,0:T(8,128)S(1)}) custom-call(s32[1]{0:T(128)} %bitcast.own_ref, bf16[1024,512]{1,0:T(8,128)(2,1)S(1)} %copy-done.4, bf16[512,128]{1,0:T(8,128)(2,1)S(1)} %copy-done.5, bf16[512,128]{1,0:T(8,128)(2,1)S(1)} %collective-permute-done.9.k2_ref, ...), custom_call_target="tpu_custom_call" | custom-call | flops 4000000000 | bytes 8000000 | tf_op jit(solution)/shard_map/stretch/pallas_call | solution.py:231
  42.9 0.0 collective-permute-done.8.far_ref
  43.0 15.3 %pages.2 = (f32[4,1024,128]{2,1,0:T(8,128)S(1)}, f32[4,1024,128]{2,1,0:T(8,128)S(1)}, f32[4,1024,128]{2,1,0:T(8,128)S(1)}) custom-call(s32[1]{0:T(128)} %bitcast.own_ref, s32[8,11]{1,0:T(8,128)S(1)} %bitcast.17, s32[2]{0:T(128)S(1)} %copy-done.7, bf16[1024,512]{1,0:T(8,128)(2,1)S(1)} %copy-done.4, ...), custom_call_target="tpu_custom_call" | custom-call | flops 4000000000 | bytes 8000000 | tf_op jit(solution)/shard_map/pages/pallas_call | solution.py:262
  58.2 0.0 collective-permute-done.2.far_ref
  58.2 10.6 %pages.3 = bf16[1024,512]{1,0:T(8,128)(2,1)} custom-call(s32[1]{0:T(128)} %bitcast.own_ref, s32[8,11]{1,0:T(8,128)S(1)} %bitcast.18, s32[2]{0:T(128)S(1)} %copy-done.7, bf16[1024,512]{1,0:T(8,128)(2,1)S(1)} %copy-done.4, bf16[2,2,256,128]{3,2,1,0:T(8,128)(2,1)S(1)} %pad_maximum_fusion.near_ref, bf16[2,2,256,128]{3,2,1,0:T(8,128)(2,1)S(1)} %collective-permute-done.2.far_ref, ...), custom_call_target="tpu_custom_call" | custom-call | flops 4000000000 | bytes 8000000 | tf_op jit(solution)/shard_map/pages/pallas_call | solution.py:262
  (17 shorter events, 0.2 us)
Async XLA Ops:
  0.0 0.9 %copy-start = (bf16[3,256,128]{2,1,0:T(8,128)(2,1)S(1)}, bf16[3,256,128]{2,1,0:T(8,128)(2,1)}, u32[]{:S(2)}) copy-start(bf16[3,256,128]{2,1,0:T(8,128)(2,1)} %keys_ref.1) | copy-start | bytes 589828
  0.9 0.9 %copy-start.1 = (bf16[3,256,128]{2,1,0:T(8,128)(2,1)S(1)}, bf16[3,256,128]{2,1,0:T(8,128)(2,1)}, u32[]{:S(2)}) copy-start(bf16[3,256,128]{2,1,0:T(8,128)(2,1)} %values_ref.1) | copy-start | bytes 589828
  1.9 0.7 copy-start.2
  2.5 35.0 %copy-start.4 = (bf16[1024,512]{1,0:T(8,128)(2,1)S(1)}, bf16[1024,512]{1,0:T(8,128)(2,1)}, u32[]{:S(2)}) copy-start(bf16[1024,512]{1,0:T(8,128)(2,1)} %q_ref.5) | copy-start | bytes 3145732
  2.5 35.0 %copy-start.5 = (bf16[512,128]{1,0:T(8,128)(2,1)S(1)}, bf16[512,128]{1,0:T(8,128)(2,1)}, u32[]{:S(2)}) copy-start(bf16[512,128]{1,0:T(8,128)(2,1)} %k_ref.1) | copy-start | bytes 393220
  2.5 35.0 %copy-start.6 = (bf16[512,128]{1,0:T(8,128)(2,1)S(1)}, bf16[512,128]{1,0:T(8,128)(2,1)}, u32[]{:S(2)}) copy-start(bf16[512,128]{1,0:T(8,128)(2,1)} %v_ref.1) | copy-start | bytes 393220
  4.9 6.1 %collective-permute-start.3 = (bf16[2,256,128]{2,1,0:T(8,128)(2,1)S(1)}, bf16[2,256,128]{2,1,0:T(8,128)(2,1)S(1)}, u32[]{:S(2)}, u32[]{:S(2)}) collective-permute-start(bf16[2,256,128]{2,1,0:T(8,128)(2,1)S(1)} %get-tuple-element.22), channel_id=1, source_target_pairs={{0,2},{1,3},{2,0},{3,1},{4,6},{5,7},{6,4},{7,5},{8,10},{9,11},{10,... | collective-permute-start | bytes 393224 | tf_op jit(solution)/shard_map/ppermute | solution.py:29
  6.2 4.8 %collective-permute-start.4 = (bf16[2,256,128]{2,1,0:T(8,128)(2,1)S(1)}, bf16[2,256,128]{2,1,0:T(8,128)(2,1)S(1)}, u32[]{:S(2)}, u32[]{:S(2)}) collective-permute-start(bf16[2,256,128]{2,1,0:T(8,128)(2,1)S(1)} %get-tuple-element.23), channel_id=1, source_target_pairs={{0,4},{1,5},{2,6},{3,7},{4,0},{5,1},{6,2},{7,3},{8,12},{9,13},{10,... | collective-permute-start | bytes 393224 | tf_op jit(solution)/shard_map/ppermute | solution.py:29
  6.3 8.6 %collective-permute-start.5 = (bf16[2,256,128]{2,1,0:T(8,128)(2,1)S(1)}, bf16[2,256,128]{2,1,0:T(8,128)(2,1)S(1)}, u32[]{:S(2)}, u32[]{:S(2)}) collective-permute-start(bf16[2,256,128]{2,1,0:T(8,128)(2,1)S(1)} %get-tuple-element.24), channel_id=1, source_target_pairs={{0,6},{1,7},{2,4},{3,5},{4,2},{5,3},{6,0},{7,1},{8,14},{9,15},{10,... | collective-permute-start | bytes 393224 | tf_op jit(solution)/shard_map/ppermute | solution.py:29
  7.6 9.0 %collective-permute-start.6 = (bf16[2,256,128]{2,1,0:T(8,128)(2,1)S(1)}, bf16[2,256,128]{2,1,0:T(8,128)(2,1)S(1)}, u32[]{:S(2)}, u32[]{:S(2)}) collective-permute-start(bf16[2,256,128]{2,1,0:T(8,128)(2,1)S(1)} %get-tuple-element.25), channel_id=1, source_target_pairs={{0,8},{1,9},{2,10},{3,11},{4,12},{5,13},{6,14},{7,15},{8,0},{9,1},... | collective-permute-start | bytes 393224 | tf_op jit(solution)/shard_map/ppermute | solution.py:29
  9.9 10.0 %collective-permute-start.7 = (bf16[2,256,128]{2,1,0:T(8,128)(2,1)S(1)}, bf16[2,256,128]{2,1,0:T(8,128)(2,1)S(1)}, u32[]{:S(2)}, u32[]{:S(2)}) collective-permute-start(bf16[2,256,128]{2,1,0:T(8,128)(2,1)S(1)} %get-tuple-element.26), channel_id=1, source_target_pairs={{0,10},{1,11},{2,8},{3,9},{4,14},{5,15},{6,12},{7,13},{8,2},{9,3},... | collective-permute-start | bytes 393224 | tf_op jit(solution)/shard_map/ppermute | solution.py:29
  20.0 23.0 %collective-permute-start.8 = (bf16[6,2,256,128]{3,2,1,0:T(8,128)(2,1)S(1)}, bf16[6,2,256,128]{3,2,1,0:T(8,128)(2,1)S(1)}, u32[]{:S(2)}, u32[]{:S(2)}) collective-permute-start(bf16[6,2,256,128]{3,2,1,0:T(8,128)(2,1)S(1)} %bitcast_dynamic-update-slice_fusion.near_ref), channel_id=1, source_target_pairs={{0,1},{1,0},{2,3},{3,2},{4,5},{5,4},{6,7},{7,6},{8,9},{9,8},{10,11... | collective-permute-start | bytes 2359304 | tf_op jit(solution)/shard_map/ppermute | solution.py:29
  22.2 5.1 %collective-permute-start = (bf16[2,256,128]{2,1,0:T(8,128)(2,1)S(1)}, bf16[2,256,128]{2,1,0:T(8,128)(2,1)S(1)}, u32[]{:S(2)}, u32[]{:S(2)}) collective-permute-start(bf16[2,256,128]{2,1,0:T(8,128)(2,1)S(1)} %get-tuple-element.19), channel_id=1, source_target_pairs={{0,12},{1,13},{2,14},{3,15},{4,8},{5,9},{6,10},{7,11},{8,4},{9,5},... | collective-permute-start | bytes 393224 | tf_op jit(solution)/shard_map/ppermute | solution.py:29
  22.2 14.4 %collective-permute-start.1 = (bf16[2,256,128]{2,1,0:T(8,128)(2,1)S(1)}, bf16[2,256,128]{2,1,0:T(8,128)(2,1)S(1)}, u32[]{:S(2)}, u32[]{:S(2)}) collective-permute-start(bf16[2,256,128]{2,1,0:T(8,128)(2,1)S(1)} %get-tuple-element.20), channel_id=1, source_target_pairs={{0,14},{1,15},{2,12},{3,13},{4,10},{5,11},{6,8},{7,9},{8,6},{9,7},... | collective-permute-start | bytes 393224 | tf_op jit(solution)/shard_map/ppermute | solution.py:29
  24.6 13.0 %collective-permute-start.10 = (bf16[512,128]{1,0:T(8,128)(2,1)}, bf16[512,128]{1,0:T(8,128)(2,1)S(1)}, u32[]{:S(2)}, u32[]{:S(2)}) collective-permute-start(bf16[512,128]{1,0:T(8,128)(2,1)} %v_ref.1), channel_id=1, source_target_pairs={{0,1},{1,0},{2,3},{3,2},{4,5},{5,4},{6,7},{7,6},{8,9},{9,8},{10,11... | collective-permute-start | bytes 393224 | tf_op jit(solution)/shard_map/ppermute | solution.py:29
  25.2 12.4 %collective-permute-start.9 = (bf16[512,128]{1,0:T(8,128)(2,1)}, bf16[512,128]{1,0:T(8,128)(2,1)S(1)}, u32[]{:S(2)}, u32[]{:S(2)}) collective-permute-start(bf16[512,128]{1,0:T(8,128)(2,1)} %k_ref.1), channel_id=1, source_target_pairs={{0,1},{1,0},{2,3},{3,2},{4,5},{5,4},{6,7},{7,6},{8,9},{9,8},{10,11... | collective-permute-start | bytes 393224 | tf_op jit(solution)/shard_map/ppermute | solution.py:29
  36.6 6.3 %copy-start.3 = (s32[2,4,11]{2,1,0:T(4,128)S(1)}, s32[2,4,11]{2,1,0:T(4,128)}, u32[]{:S(2)}) copy-start(s32[2,4,11]{2,1,0:T(4,128)} %param.13) | copy-start | bytes 1060
  36.6 6.3 %copy-start.7 = (s32[2]{0:T(128)S(1)}, s32[2]{0:T(128)}, u32[]{:S(2)}) copy-start(s32[2]{0:T(128)} %counts_ref.3) | copy-start | bytes 28
  36.6 21.6 %collective-permute-start.2 = (bf16[2,2,256,128]{3,2,1,0:T(8,128)(2,1)S(1)}, bf16[2,2,256,128]{3,2,1,0:T(8,128)(2,1)S(1)}, u32[]{:S(2)}, u32[]{:S(2)}) collective-permute-start(bf16[2,2,256,128]{3,2,1,0:T(8,128)(2,1)S(1)} %pad_maximum_fusion.near_ref), channel_id=1, source_target_pairs={{0,1},{1,0},{2,3},{3,2},{4,5},{5,4},{6,7},{7,6},{8,9},{9,8},{10,11... | collective-permute-start | bytes 786440 | tf_op jit(solution)/shard_map/ppermute | solution.py:29
